TPU v7x, 128 devices: a whole 4x4x4 slice. The times are simulated.
128 devices in a mesh: row: 16 (over z_hi, y, core), col: 8 (over z_lo, x).
Axes of the slice: x: 4, y: 4, z: 4 (z_hi: 2, z_lo: 2; z = z_hi * 2 + z_lo), core: 2. Of those that a mesh axis runs over, the one named last changes fastest.
Arguments:
- tiles: bfloat16 [128, 128, 1536], P('row', 'col'), may hold values from -6 to 6
- tissue: int32 [128, 128], P('row', 'col'), may hold values from 0 to 1, as said below
- project_in: bfloat16 [1536, 2304], P(('row', 'col')), as said below
- project_out: bfloat16 [768, 1536], P(('row', 'col')), may hold values from -0.21875 to 0.21875
- grad_layer: bfloat16 [128, 128, 1536], P('row', 'col'), may hold values from -6 to 6
Outputs:
- layer_out: bfloat16 [128, 128, 1536], P('row', 'col')
- grad_tiles: bfloat16 [128, 128, 1536], P('row', 'col')
- grad_project_in: float32 [1536, 2304], P(('row', 'col'))
- grad_project_out: float32 [768, 1536], P(('row', 'col'))
Inputs may be any that keep to these rules, and one draw needn't show every extreme that they name: 1 marks a tissue tile, 0 a background tile; tissue lies in patches. `project_in`: query, key and value projections side by side along the second dimension.
All inputs are finite; a program needn't handle non-finite values.
Results may differ from a plain program's by a relative error of at most 0.009.
Values may be sent and summed in bfloat16 or wider, within the bound.
No kernel may reach another device: no remote copies, remote signals or barrier semaphores. Data moves between devices by JAX's collectives and lax.ppermute only.
A program may use at most 128 MiB of HBM per device.

v0:
```python
import jax
import jax.numpy as jnp
from jax import lax
from jax.sharding import PartitionSpec as P

HEADS = 12
HEAD_DIM = 64
WINDOW = 7
DH = 768


epsilon = 1e-05
masked_score = -1e30
outside_score = -3e30


def from_behind(value, axis, steps):
    count = lax.axis_size(axis)
    first, last = (max(0, -steps), min(count, count - steps))
    return lax.ppermute(value, axis, [(source, source + steps) for source in range(first, last)])


def as_sent(value):

    def short(part):
        return part.astype(jnp.bfloat16) if part.dtype == jnp.float32 else part

    return jax.tree.map(short, value)


def extended(value, sides, width):
    for axis, dim in sides:
        devices, length = (lax.axis_size(axis), value.shape[dim])
        up = [(i, (i + 1) % devices) for i in range(devices - 1)]
        down = [(j, i) for i, j in up]
        last = lax.slice_in_dim(value, length - width, length, axis=dim)
        first = lax.slice_in_dim(value, 0, width, axis=dim)
        before = lax.ppermute(last, axis, up)
        after = lax.ppermute(first, axis, down)
        value = jnp.concatenate([before, value, after], axis=dim)
    return value


def normalize(values):
    center = values - jnp.mean(values, axis=-1, keepdims=True)
    inverse = lax.rsqrt(jnp.mean(center * center, axis=-1, keepdims=True) + epsilon)
    return (center * inverse, inverse)


def fold_cols(gradient):
    margin = WINDOW // 2
    inner = gradient[:, margin:-margin]
    from_right = from_behind(gradient[:, :margin].astype(jnp.bfloat16), "col", -1).astype(
        jnp.float32
    )
    from_left = from_behind(gradient[:, -margin:].astype(jnp.bfloat16), "col", 1).astype(
        jnp.float32
    )
    first_part = inner[:, :margin] + from_left
    last_part = inner[:, -margin:] + from_right
    return jnp.concatenate([first_part, inner[:, margin:-margin], last_part], axis=1)


def fold_rows(gradient):
    margin = WINDOW // 2
    inner = gradient[margin:-margin]
    from_below = from_behind(as_sent(gradient[:margin]), "row", -1)
    from_above = from_behind(as_sent(gradient[-margin:]), "row", 1)
    first_part = inner[:margin] + from_above
    last_part = inner[-margin:] + from_below
    return jnp.concatenate([first_part, inner[margin:-margin], last_part], axis=0)


def window_lines(count, base, total, padded_count):
    margin = WINDOW // 2
    query_place = base + jnp.arange(count, dtype=jnp.int32)
    start = jnp.clip(query_place - margin, 0, total - WINDOW)
    key_place = base - margin + jnp.arange(padded_count, dtype=jnp.int32)
    return jnp.logical_and(
        key_place[None, :] >= start[:, None], key_place[None, :] < start[:, None] + WINDOW
    )


def body(tiles, tissue, project_in, project_out, grad_layer):
    height, breadth, model_width = tiles.shape
    tokens = height * breadth
    margin = WINDOW // 2
    scale = HEAD_DIM ** (-0.5)
    flat_tiles = tiles.reshape(tokens, model_width).astype(jnp.float32)
    normed, inverse = normalize(flat_tiles)
    hidden = normed.astype(jnp.bfloat16)
    input_whole = lax.all_gather(project_in, ("row", "col"), axis=0, tiled=True)
    output_whole = lax.all_gather(project_out, ("row", "col"), axis=0, tiled=True)
    projected_in = jnp.dot(hidden, input_whole, preferred_element_type=jnp.float32)
    packed = projected_in.astype(jnp.bfloat16)
    query = packed[:, :DH]
    pairs = packed[:, DH:].reshape(height, breadth, 2 * DH)
    padded = extended(pairs, (("row", 0), ("col", 1)), margin)
    live_pad = extended(tissue, (("row", 0), ("col", 1)), margin)
    pad_high = height + 2 * margin
    pad_wide = breadth + 2 * margin
    places = pad_high * pad_wide
    key_flat = padded[:, :, :DH].reshape(places, DH)
    value_flat = padded[:, :, DH:].reshape(places, DH)
    row_in = window_lines(
        height, lax.axis_index("row") * height, lax.axis_size("row") * height, pad_high
    )
    col_in = window_lines(
        breadth, lax.axis_index("col") * breadth, lax.axis_size("col") * breadth, pad_wide
    )
    inside = jnp.logical_and(row_in[:, None, :, None], col_in[None, :, None, :]).reshape(
        tokens, places
    )
    alive = live_pad.reshape(1, places) > 0
    groups = HEADS // 2
    pair_width = 2 * HEAD_DIM

    def by_group(values):
        return values.reshape(values.shape[0], groups, pair_width).transpose(1, 0, 2)

    def split_heads(values):
        return values.reshape(values.shape[0], 2, HEAD_DIM)

    def probabilities(query_pair, key_pair):
        raw = (
            jnp.einsum(
                "qhd,khd->hqk",
                split_heads(query_pair),
                split_heads(key_pair),
                preferred_element_type=jnp.float32,
            )
            * scale
        )
        scores = jnp.where(inside[None], jnp.where(alive[None], raw, masked_score), outside_score)
        highest = jnp.max(scores, axis=-1, keepdims=True)
        expon = jnp.exp(scores - highest)
        return expon / jnp.sum(expon, axis=-1, keepdims=True)

    def forward_pair(operands):
        query_pair, key_pair, value_pair = operands
        weights = probabilities(query_pair, key_pair).astype(jnp.bfloat16)
        mixed = jnp.einsum(
            "hqk,khd->qhd", weights, split_heads(value_pair), preferred_element_type=jnp.float32
        )
        return mixed.astype(jnp.bfloat16).reshape(tokens, pair_width)

    query_groups = by_group(query)
    key_groups = by_group(key_flat)
    value_groups = by_group(value_flat)
    attention_groups = lax.map(forward_pair, (query_groups, key_groups, value_groups))
    attention = attention_groups.transpose(1, 0, 2).reshape(tokens, DH)
    projected = jnp.dot(attention, output_whole, preferred_element_type=jnp.float32)
    live = tissue.reshape(tokens, 1).astype(jnp.float32)
    layer_out = (
        (flat_tiles + projected * live).astype(jnp.bfloat16).reshape(height, breadth, model_width)
    )
    grad_flat = grad_layer.reshape(tokens, model_width).astype(jnp.float32)
    grad_proj = (grad_flat * live).astype(jnp.bfloat16)
    block = attention
    grad_project_out = lax.psum_scatter(
        lax.dot_general(
            block, grad_proj, (((0,), (0,)), ((), ())), preferred_element_type=jnp.float32
        ),
        ("row", "col"),
        scatter_dimension=0,
        tiled=True,
    )
    grad_attention = lax.dot_general(
        grad_proj, output_whole, (((1,), (1,)), ((), ())), preferred_element_type=jnp.float32
    ).astype(jnp.bfloat16)

    def backward_pair(operands):
        query_pair, key_pair, value_pair, grad_pair, attention_pair = operands
        prob = probabilities(query_pair, key_pair)
        weights = prob.astype(jnp.bfloat16)
        grad_heads = split_heads(grad_pair)
        delta = jnp.einsum(
            "qhd,qhd->hq",
            grad_heads,
            split_heads(attention_pair),
            preferred_element_type=jnp.float32,
        )
        grad_prob = jnp.einsum(
            "qhd,khd->hqk", grad_heads, split_heads(value_pair), preferred_element_type=jnp.float32
        )
        grad_score = prob * (grad_prob - delta[:, :, None]) * scale
        grad_q = jnp.einsum(
            "hqk,khd->qhd",
            grad_score,
            split_heads(key_pair).astype(jnp.float32),
            precision=lax.Precision.HIGHEST,
        )
        grad_k = jnp.einsum(
            "hqk,qhd->khd",
            grad_score,
            split_heads(query_pair).astype(jnp.float32),
            precision=lax.Precision.HIGHEST,
        )
        grad_v = jnp.einsum("hqk,qhd->khd", weights, grad_heads, preferred_element_type=jnp.float32)
        return (
            grad_q.reshape(tokens, pair_width),
            grad_k.reshape(places, pair_width),
            grad_v.reshape(places, pair_width),
        )

    grad_q_groups, grad_k_groups, grad_v_groups = lax.map(
        backward_pair,
        (query_groups, key_groups, value_groups, by_group(grad_attention), attention_groups),
    )
    grad_query = grad_q_groups.transpose(1, 0, 2).reshape(tokens, DH)
    grad_keys = grad_k_groups.transpose(1, 0, 2).reshape(pad_high, pad_wide, DH)
    grad_values = grad_v_groups.transpose(1, 0, 2).reshape(pad_high, pad_wide, DH)
    grad_pairs = jnp.concatenate([grad_keys, grad_values], axis=-1)
    own_pairs = fold_rows(fold_cols(grad_pairs))
    grad_packed = jnp.concatenate([grad_query, own_pairs.reshape(tokens, 2 * DH)], axis=-1).astype(
        jnp.bfloat16
    )
    block = hidden
    grad_project_in = lax.psum_scatter(
        lax.dot_general(
            block, grad_packed, (((0,), (0,)), ((), ())), preferred_element_type=jnp.float32
        ),
        ("row", "col"),
        scatter_dimension=0,
        tiled=True,
    )
    grad_hidden = lax.dot_general(
        grad_packed,
        lax.all_gather(project_in, ("row", "col"), axis=0, tiled=True),
        (((1,), (1,)), ((), ())),
        preferred_element_type=jnp.float32,
    )
    grad_norm = inverse * (
        grad_hidden
        - jnp.mean(grad_hidden, axis=-1, keepdims=True)
        - normed * jnp.mean(grad_hidden * normed, axis=-1, keepdims=True)
    )
    grad_tiles = (grad_flat + grad_norm).astype(jnp.bfloat16).reshape(height, breadth, model_width)
    return (layer_out, grad_tiles, grad_project_in, grad_project_out)


def solution(mesh):
    placed = (
        P("row", "col", None),
        P("row", "col"),
        P(("row", "col"), None),
        P(("row", "col"), None),
        P("row", "col", None),
    )
    return jax.shard_map(
        body,
        mesh=mesh,
        in_specs=placed,
        out_specs=(
            P("row", "col", None),
            P("row", "col", None),
            P(("row", "col"), None),
            P(("row", "col"), None),
        ),
        check_vma=False,
    )
```

profile of v0, /device:TPU:1, one launch (start us, length us, event | category | flops | bytes accessed | tf_op | source)
XLA Modules:
  0.0 1514.5 jit_solution(3303132193105354588)
XLA Ops:
  22.7 307.6 %all-gather.5.cloned.1.call-done = bf16[128,12,2304]{2,1,0:T(8,128)(2,1)} async-done(((bf16[1,12,2304]{2,1,0:T(8,128)(2,1)}), bf16[128,12,2304]{2,1,0:T(8,128)(2,1)}) %all-gather.5.cloned.1.call-update) | async-done | bytes 7077904 | tf_op jit(solution)/shard_map/all_gather | solution.py:92
  330.3 11.2 reshape.316
  359.0 278.3 %all-gather.7.cloned.1.call-done = bf16[128,6,1536]{2,1,0:T(8,128)(2,1)} async-done(((bf16[1,6,1536]{2,1,0:T(8,128)(2,1)}), bf16[128,6,1536]{2,1,0:T(8,128)(2,1)}) %all-gather.7.cloned.1.call-update) | async-done | bytes 2359312 | tf_op jit(solution)/shard_map/all_gather | solution.py:93
  645.1 4.7 collective-permute-start.2
  665.3 35.4 %while.26 = (s32[]{:T(128)}, bf16[6,128,128]{1,2,0:T(8,128)(2,1)}, bf16[6,308,128]{1,2,0:T(8,128)(2,1)}, pred[1,308]{1,0:T(4,128)(4,1)S(1)}, bf16[6,128,128]{1,2...) while((s32[]{:T(128)}, bf16[6,128,128]{1,2,0:T(8,128)(2,1)}, ...), condition=%wide.region_5.6_spmd.clone, body=%wide.region_2.5_spmd.clone.sunk | while | flops 31201640 | bytes 1691930 | solution.py:150
  700.8 70.0 %while.27 = (s32[]{:T(128)}, bf16[6,128,128]{1,2,0:T(8,128)(2,1)}, f32[6,308,128]{1,2,0:T(8,128)}, f32[6,308,128]{1,2,0:T(8,128)}, bf16[6,308,128]{1,2,0:T(8,128...) while((s32[]{:T(128)}, bf16[6,128,128]{1,2,0:T(8,128)(2,1)}, ...), condition=%wide.region_9.10_spmd.clone, body=%wide.region_6.9_spmd.clone.sunk | while | flops 162768992 | bytes 4669770 | solution.py:206
  787.9 4.1 collective-permute-start.8
  801.4 4.2 collective-permute-start.10
  814.5 7.0 fusion.36
  821.5 370.9 %fusion.43 = (f32[16,2304]{1,0:T(8,128)S(1)}, f32[8,1536]{1,0:T(8,128)}) fusion(f32[1536,2304]{1,0:T(8,128)} %fusion.36, f32[768,1536]{1,0:T(8,128)} %fusion.55), kind=kCustom, calls=%all-reduce-scatter.2 | all-reduce-scatter fusion | flops 6291458 | bytes 19070976
  1198.5 24.8 %collective-permute-start.71 = (f32[8,1536]{1,0:T(8,128)}, f32[8,1536]{1,0:T(8,128)S(1)}, u32[]{:S(2)}, u32[]{:S(2)}) collective-permute-start(f32[8,1536]{1,0:T(8,128)} %get-tuple-element.269), channel_id=1, source_target_pairs={{0,28},{1,29},{2,30},{3,31},{4,32},{5,33},{6,34},{7,35},{8,36},{9,... | collective-permute-start | bytes 147464
  1223.4 5.9 collective-permute-start.70
  1294.8 4.3 collective-permute-start.45
  1305.1 5.7 collective-permute-done.44
  1320.7 6.0 collective-permute-done.39
  1326.7 4.6 collective-permute-start.34
  1333.6 6.3 collective-permute-start.32
  1339.9 5.5 fusion.42
  1356.1 9.6 collective-permute-start.26
  1365.8 5.7 collective-permute-start.25
  1377.0 9.6 collective-permute-start.21
  1398.7 29.7 %concatenate.35 = f32[262,1536]{1,0:T(8,128)S(1)} concatenate(f32[6,1536]{1,0:T(8,128)} %copy-done.47, f32[8,1536]{1,0:T(8,128)} %copy-done.46, f32[8,1536]{1,0:T(8,128)} %copy-done.48, f32[8,1536]{1,0:T(8,128)} %copy-done.49, f32[8,1536]{1,0:T(8,128)} %copy-done.50, f32[8,1536]{1,0:T(8,128)} %copy-done.51, f32[8,1536]{1,0:T(8,128)} %copy-done.52, f32[8,1536]{1,0:T(8,128)} %copy-done.53, ...), dimensions={0} | concatenate | bytes 3219456
  1439.7 5.7 collective-permute-start.12
  1450.3 55.8 %concatenate.34 = f32[524,2304]{1,0:T(8,128)} concatenate(f32[12,2304]{1,0:T(8,128)} %collective-permute-done.43, f32[16,2304]{1,0:T(8,128)} %collective-permute-done.42, f32[16,2304]{1,0:T(8,128)S(1)} %copy-done.13, f32[16,2304]{1,0:T(8,128)S(1)} %copy-done.15, f32[16,2304]{1,0:T(8,128)S(1)} %copy-done.17, f32[16,2304]{1,0:T(8,128)S(1)} %copy-done.19, ...), dimensions={0} | concatenate | bytes 9658368
  (513 shorter events, 330.9 us)
Async XLA Ops:
  7.2 323.1 %all-gather.5.cloned.1.call-start = ((), (), s32[]{:S(2)}) async-start(), calls=%async_computation | async-start | bytes 9510912 | tf_op jit(solution)/shard_map/all_gather | solution.py:92
  7.9 629.4 %all-gather.7.cloned.1.call-start = ((), (), s32[]{:S(2)}) async-start(), calls=%async_computation.1 | async-start | bytes 3170304 | tf_op jit(solution)/shard_map/all_gather | solution.py:93
  347.2 294.9 %collective-permute-start.1 = (bf16[3,16,1536]{2,1,0:T(8,128)(2,1)}, bf16[3,16,1536]{2,1,0:T(8,128)(2,1)S(1)}, u32[]{:S(2)}, u32[]{:S(2)}) collective-permute-start(bf16[3,16,1536]{2,1,0:T(8,128)(2,1)} %bitcast.6), channel_id=1, source_target_pairs={{8,0},{16,8},{24,16},{32,24},{40,32},{48,40},{56,48},{64,56},{72,6... | collective-permute-start | bytes 442376 | tf_op jit(solution)/shard_map/ppermute | solution.py:39
  349.1 293.0 %collective-permute-start = (bf16[3,16,1536]{2,1,0:T(8,128)(2,1)}, bf16[3,16,1536]{2,1,0:T(8,128)(2,1)S(1)}, u32[]{:S(2)}, u32[]{:S(2)}) collective-permute-start(bf16[3,16,1536]{2,1,0:T(8,128)(2,1)} %bitcast.4), channel_id=1, source_target_pairs={{0,8},{8,16},{16,24},{24,32},{32,40},{40,48},{48,56},{56,64},{64,7... | collective-permute-start | bytes 442376 | tf_op jit(solution)/shard_map/ppermute | solution.py:38
  1192.4 36.9 %collective-permute-start.74 = (f32[8,1536]{1,0:T(8,128)}, f32[8,1536]{1,0:T(8,128)S(1)}, u32[]{:S(2)}, u32[]{:S(2)}) collective-permute-start(f32[8,1536]{1,0:T(8,128)} %get-tuple-element.269), channel_id=1, source_target_pairs={{0,31},{1,32},{2,33},{3,34},{4,35},{5,36},{6,37},{7,38},{8,39},{9,... | collective-permute-start | bytes 147464
  1194.6 28.7 %collective-permute-start.75 = (f32[6,1536]{1,0:T(8,128)S(1)}, f32[6,1536]{1,0:T(8,128)S(1)}, u32[]{:S(2)}, u32[]{:S(2)}) collective-permute-start(f32[6,1536]{1,0:T(8,128)S(1)} %slice.130), channel_id=1, source_target_pairs={{0,32},{1,33},{2,34},{3,35},{4,36},{5,37},{6,38},{7,39},{8,40},{9,... | collective-permute-start | bytes 110600
  1195.9 35.6 %collective-permute-start.73 = (f32[8,1536]{1,0:T(8,128)}, f32[8,1536]{1,0:T(8,128)S(1)}, u32[]{:S(2)}, u32[]{:S(2)}) collective-permute-start(f32[8,1536]{1,0:T(8,128)} %get-tuple-element.269), channel_id=1, source_target_pairs={{0,30},{1,31},{2,32},{3,33},{4,34},{5,35},{6,36},{7,37},{8,38},{9,... | collective-permute-start | bytes 147464
  1197.2 35.6 %collective-permute-start.72 = (f32[8,1536]{1,0:T(8,128)}, f32[8,1536]{1,0:T(8,128)S(1)}, u32[]{:S(2)}, u32[]{:S(2)}) collective-permute-start(f32[8,1536]{1,0:T(8,128)} %get-tuple-element.269), channel_id=1, source_target_pairs={{0,29},{1,30},{2,31},{3,32},{4,33},{5,34},{6,35},{7,36},{8,37},{9,... | collective-permute-start | bytes 147464
  1198.5 35.6 %collective-permute-start.71 = (f32[8,1536]{1,0:T(8,128)}, f32[8,1536]{1,0:T(8,128)S(1)}, u32[]{:S(2)}, u32[]{:S(2)}) collective-permute-start(f32[8,1536]{1,0:T(8,128)} %get-tuple-element.269), channel_id=1, source_target_pairs={{0,28},{1,29},{2,30},{3,31},{4,32},{5,33},{6,34},{7,35},{8,36},{9,... | collective-permute-start | bytes 147464
  1279.6 33.9 %collective-permute-start.42 = (f32[16,2304]{1,0:T(8,128)S(1)}, f32[16,2304]{1,0:T(8,128)}, u32[]{:S(2)}, u32[]{:S(2)}) collective-permute-start(f32[16,2304]{1,0:T(8,128)S(1)} %get-tuple-element.268), channel_id=1, source_target_pairs={{0,31},{1,32},{2,33},{3,34},{4,35},{5,36},{6,37},{7,38},{8,39},{9,... | collective-permute-start | bytes 442376
  1282.2 29.9 %collective-permute-start.43 = (f32[12,2304]{1,0:T(8,128)}, f32[12,2304]{1,0:T(8,128)}, u32[]{:S(2)}, u32[]{:S(2)}) collective-permute-start(f32[12,2304]{1,0:T(8,128)} %slice.129), channel_id=1, source_target_pairs={{0,32},{1,33},{2,34},{3,35},{4,36},{5,37},{6,38},{7,39},{8,40},{9,... | collective-permute-start | bytes 331784
  1317.0 28.4 %collective-permute-start.36 = (f32[16,2304]{1,0:T(8,128)S(1)}, f32[16,2304]{1,0:T(8,128)S(1)}, u32[]{:S(2)}, u32[]{:S(2)}) collective-permute-start(f32[16,2304]{1,0:T(8,128)S(1)} %get-tuple-element.268), channel_id=1, source_target_pairs={{0,25},{1,26},{2,27},{3,28},{4,29},{5,30},{6,31},{7,32},{8,33},{9,... | collective-permute-start | bytes 442376
  1318.4 29.5 %collective-permute-start.35 = (f32[16,2304]{1,0:T(8,128)S(1)}, f32[16,2304]{1,0:T(8,128)S(1)}, u32[]{:S(2)}, u32[]{:S(2)}) collective-permute-start(f32[16,2304]{1,0:T(8,128)S(1)} %get-tuple-element.268), channel_id=1, source_target_pairs={{0,24},{1,25},{2,26},{3,27},{4,28},{5,29},{6,30},{7,31},{8,32},{9,... | collective-permute-start | bytes 442376
  1326.7 24.4 %collective-permute-start.34 = (f32[16,2304]{1,0:T(8,128)S(1)}, f32[16,2304]{1,0:T(8,128)S(1)}, u32[]{:S(2)}, u32[]{:S(2)}) collective-permute-start(f32[16,2304]{1,0:T(8,128)S(1)} %get-tuple-element.268), channel_id=1, source_target_pairs={{0,23},{1,24},{2,25},{3,26},{4,27},{5,28},{6,29},{7,30},{8,31},{9,... | collective-permute-start | bytes 442376
  1331.3 21.9 %collective-permute-start.33 = (f32[16,2304]{1,0:T(8,128)S(1)}, f32[16,2304]{1,0:T(8,128)S(1)}, u32[]{:S(2)}, u32[]{:S(2)}) collective-permute-start(f32[16,2304]{1,0:T(8,128)S(1)} %get-tuple-element.268), channel_id=1, source_target_pairs={{0,22},{1,23},{2,24},{3,25},{4,26},{5,27},{6,28},{7,29},{8,30},{9,... | collective-permute-start | bytes 442376
  1333.6 21.0 %collective-permute-start.32 = (f32[16,2304]{1,0:T(8,128)S(1)}, f32[16,2304]{1,0:T(8,128)S(1)}, u32[]{:S(2)}, u32[]{:S(2)}) collective-permute-start(f32[16,2304]{1,0:T(8,128)S(1)} %get-tuple-element.268), channel_id=1, source_target_pairs={{0,21},{1,22},{2,23},{3,24},{4,25},{5,26},{6,27},{7,28},{8,29},{9,... | collective-permute-start | bytes 442376
  1356.1 20.9 %collective-permute-start.26 = (f32[16,2304]{1,0:T(8,128)S(1)}, f32[16,2304]{1,0:T(8,128)S(1)}, u32[]{:S(2)}, u32[]{:S(2)}) collective-permute-start(f32[16,2304]{1,0:T(8,128)S(1)} %get-tuple-element.268), channel_id=1, source_target_pairs={{0,15},{1,16},{2,17},{3,18},{4,19},{5,20},{6,21},{7,22},{8,23},{9,... | collective-permute-start | bytes 442376
  1365.8 20.8 %collective-permute-start.25 = (f32[16,2304]{1,0:T(8,128)S(1)}, f32[16,2304]{1,0:T(8,128)S(1)}, u32[]{:S(2)}, u32[]{:S(2)}) collective-permute-start(f32[16,2304]{1,0:T(8,128)S(1)} %get-tuple-element.268), channel_id=1, source_target_pairs={{0,14},{1,15},{2,16},{3,17},{4,18},{5,19},{6,20},{7,21},{8,22},{9,... | collective-permute-start | bytes 442376
  1374.2 20.7 %collective-permute-start.22 = (f32[16,2304]{1,0:T(8,128)S(1)}, f32[16,2304]{1,0:T(8,128)S(1)}, u32[]{:S(2)}, u32[]{:S(2)}) collective-permute-start(f32[16,2304]{1,0:T(8,128)S(1)} %get-tuple-element.268), channel_id=1, source_target_pairs={{0,11},{1,12},{2,13},{3,14},{4,15},{5,16},{6,17},{7,18},{8,19},{9,... | collective-permute-start | bytes 442376
  1377.0 51.4 %collective-permute-start.21 = (f32[16,2304]{1,0:T(8,128)S(1)}, f32[16,2304]{1,0:T(8,128)}, u32[]{:S(2)}, u32[]{:S(2)}) collective-permute-start(f32[16,2304]{1,0:T(8,128)S(1)} %get-tuple-element.268), channel_id=1, source_target_pairs={{0,10},{1,11},{2,12},{3,13},{4,14},{5,15},{6,16},{7,17},{8,18},{9,... | collective-permute-start | bytes 442376
  1386.6 44.9 %collective-permute-start.20 = (f32[16,2304]{1,0:T(8,128)S(1)}, f32[16,2304]{1,0:T(8,128)}, u32[]{:S(2)}, u32[]{:S(2)}) collective-permute-start(f32[16,2304]{1,0:T(8,128)S(1)} %get-tuple-element.268), channel_id=1, source_target_pairs={{0,9},{1,10},{2,11},{3,12},{4,13},{5,14},{6,15},{7,16},{8,17},{9,1... | collective-permute-start | bytes 442376
  1389.8 43.6 %collective-permute-start.19 = (f32[16,2304]{1,0:T(8,128)S(1)}, f32[16,2304]{1,0:T(8,128)}, u32[]{:S(2)}, u32[]{:S(2)}) collective-permute-start(f32[16,2304]{1,0:T(8,128)S(1)} %get-tuple-element.268), channel_id=1, source_target_pairs={{0,8},{1,9},{2,10},{3,11},{4,12},{5,13},{6,14},{7,15},{8,16},{9,17... | collective-permute-start | bytes 442376
  1391.8 44.5 %collective-permute-start.18 = (f32[16,2304]{1,0:T(8,128)S(1)}, f32[16,2304]{1,0:T(8,128)}, u32[]{:S(2)}, u32[]{:S(2)}) collective-permute-start(f32[16,2304]{1,0:T(8,128)S(1)} %get-tuple-element.268), channel_id=1, source_target_pairs={{0,7},{1,8},{2,9},{3,10},{4,11},{5,12},{6,13},{7,14},{8,15},{9,16}... | collective-permute-start | bytes 442376
  1394.9 44.7 %collective-permute-start.17 = (f32[16,2304]{1,0:T(8,128)S(1)}, f32[16,2304]{1,0:T(8,128)}, u32[]{:S(2)}, u32[]{:S(2)}) collective-permute-start(f32[16,2304]{1,0:T(8,128)S(1)} %get-tuple-element.268), channel_id=1, source_target_pairs={{0,6},{1,7},{2,8},{3,9},{4,10},{5,11},{6,12},{7,13},{8,14},{9,15},... | collective-permute-start | bytes 442376
  (123 other events, 3113.5 us)
Sparse Core Ops, SparseCore 0:
  9.7 320.5 all-gather.4
  332.0 305.2 all-gather.6
where the time goes:
time: 1530 us; the launch traced here: 1510 us
  waiting for transfers between devices  609 us (40%)
  blocking collectives  371 us (24%)
  starting transfers between devices  234 us (15%)
  local copies, waits for them, and re-layouts  196 us (13%)
  matrix products  71.5 us (5%)
  other arithmetic  17.3 us (1%)
  between operations  16.1 us (1%)
    unnamed x1, blocking collectives  371 us
    all_gather x1, waiting for transfers between devices, body(): input_whole = lax.all_gather(project_in, ('row', 'col'), axis=0, tiled=True)  308 us
    all_gather x1, waiting for transfers between devices, body(): lax.all_gather(project_out, ('row', 'col'), axis=0, tiled=True)  278 us
    unnamed x64, starting transfers between devices  198 us
    unnamed x147, local copies, waits for them, and re-layouts  116 us
    dynamic_slice x42, local copies, waits for them, and re-layouts, body(): lax.map(forward_pair, (query_groups, key_groups, value_groups))  35 us
  transfers between devices with their start and end apart: 78, of which 9 were waited for; matrix products, arithmetic and copies ran while one was open for 5% of the time, Pallas kernels for 0%

commit v1 on v0

v1 whole, which is shorter than its diff:
```python
import jax
import jax.numpy as jnp
from jax import lax
from jax.experimental import pallas as pl
from jax.experimental.pallas import tpu as pltpu
from jax.sharding import Mesh, PartitionSpec as P

HEAD_DIM = 64
WINDOW = 7
D = 1536
DH = 768
HALF = DH // 2
GRID = 128
SIDE = 16
KEY_ROWS = 28
KEY_COLS = 32
QUERY_ROWS = 22
QUERY_COLS = 24
LANE = 128

AXES = ("zh", "y", "c", "zl", "x")
STAGES = (("z", "y", "x"), ("x", "z", "y"))

epsilon = 1e-05
masked_score = -1e30
outside_score = -3e30
open_score = 3e38

f32 = jnp.float32
bf16 = jnp.bfloat16


def device(x, y, z, c):
    return (((z // 2 * 4 + y) * 2 + c) * 2 + z % 2) * 4 + x


def stage_pairs(stage, shift):
    pairs = []
    for x in range(4):
        for y in range(4):
            for z in range(4):
                for c in range(2):
                    place = {"x": x, "y": y, "z": z}
                    axis = STAGES[c][stage]
                    place[axis] = (place[axis] + shift) % 4
                    pairs.append((device(x, y, z, c), device(place["x"], place["y"], place["z"], c)))
    return pairs


def shifted(value, stage, shift):
    return lax.ppermute(value, AXES, stage_pairs(stage, shift))


def swap_cores(value):
    return lax.ppermute(value, "c", [(0, 1), (1, 0)])


def row_neighbour(value):
    pairs = [(r, r + 1 if r % 2 else r - 1) for r in range(16)]
    return lax.ppermute(value, ("zh", "y", "c"), [(a, b) for a, b in pairs if 0 <= b < 16])


def col_neighbour(value, step):
    pairs = [(i, i + step) for i in range(8)]
    return lax.ppermute(value, ("zl", "x"), [(a, b) for a, b in pairs if 0 <= b < 8])


def gather_stage(block, stage):
    far = shifted(block, stage, 2)
    near = shifted(block, stage, 1)
    back = shifted(block, stage, 3)
    return [block, near, far, back]


def scatter_stage(chunks, stage):
    far = shifted(chunks[2], stage, 2)
    near = shifted(chunks[1], stage, 3)
    back = shifted(chunks[3], stage, 1)
    return (chunks[0].astype(f32) + near.astype(f32)) + (far.astype(f32) + back.astype(f32))


def by_core(core, mine, other, axis):
    return jnp.where(
        core == 0,
        jnp.concatenate([mine, other], axis=axis),
        jnp.concatenate([other, mine], axis=axis),
    )


def normalize(values):
    center = values - jnp.mean(values, axis=-1, keepdims=True)
    inverse = lax.rsqrt(jnp.mean(center * center, axis=-1, keepdims=True) + epsilon)
    return (center * inverse, inverse)


def attention_kernel(base_ref, packed_ref, grad_ref, alive_ref, col_ref, attn_out, grads_out, dk, dv, attn, dq):
    base = base_ref[0]
    width = 2 * QUERY_COLS
    span = 8 * KEY_COLS
    dk[...] = jnp.zeros_like(dk)
    dv[...] = jnp.zeros_like(dv)
    key_line = lax.broadcasted_iota(jnp.int32, (1, span), 1) // KEY_COLS
    low = lax.broadcasted_iota(jnp.int32, (width, LANE), 1) < HEAD_DIM
    low2 = jnp.concatenate([low, jnp.logical_not(low)], axis=0)

    def block(i, carry):
        row = base - 3 + 2 * i
        start = jnp.clip(row - 3, 0, GRID - 8)
        local = start - (base - 6)
        alive = alive_ref[pl.ds(local, 1), :]
        key_row = key_line + start
        caps = []
        for step in range(2):
            first = jnp.clip(row + step - 3, 0, GRID - WINDOW)
            inside = jnp.logical_and(key_row >= first, key_row < first + WINDOW)
            caps.append(jnp.minimum(col_ref[...], jnp.where(inside, alive, outside_score)))
        cap = jnp.concatenate(caps + caps, axis=0)
        keys_at = pl.ds(pl.multiple_of(local * KEY_COLS, KEY_COLS), span)
        query_at = pl.multiple_of((3 + 2 * i) * KEY_COLS, KEY_COLS)
        block_at = pl.ds(pl.multiple_of(i * width, width), width)
        for g in range(3):
            q_lanes = pl.ds(g * LANE, LANE)
            k_lanes = pl.ds(HALF + g * LANE, LANE)
            v_lanes = pl.ds(2 * HALF + g * LANE, LANE)
            key = packed_ref[keys_at, k_lanes]
            value = packed_ref[keys_at, v_lanes]
            lines = packed_ref[pl.ds(query_at, 2 * KEY_COLS), q_lanes].astype(f32) * HEAD_DIM ** (-0.5)
            query = jnp.concatenate([lines[:QUERY_COLS], lines[KEY_COLS : KEY_COLS + QUERY_COLS]], axis=0)
            grad = grad_ref[block_at, q_lanes].astype(f32)
            query2 = jnp.where(low2, jnp.concatenate([query, query], axis=0), 0.0).astype(bf16)
            grad2f = jnp.where(low2, jnp.concatenate([grad, grad], axis=0), 0.0)
            grad2 = grad2f.astype(bf16)
            contract = (((1,), (1,)), ((), ()))
            raw = lax.dot_general(query2, key, contract, preferred_element_type=f32)
            scores = jnp.minimum(raw, cap)
            expon = jnp.exp(scores - jnp.max(scores, axis=1, keepdims=True))
            prob = expon * (1.0 / jnp.sum(expon, axis=1, keepdims=True))
            weights = prob.astype(bf16)
            mixed2 = jnp.dot(weights, value, preferred_element_type=f32).astype(bf16).astype(f32)
            attn[block_at, q_lanes] = jnp.where(low, mixed2[:width], mixed2[width:])
            delta = jnp.sum(grad2f * mixed2, axis=1, keepdims=True)
            grad_prob = lax.dot_general(grad2, value, contract, preferred_element_type=f32)
            grad_score = (prob * (grad_prob - delta)).astype(bf16)
            grad_q = jnp.dot(grad_score, key, preferred_element_type=f32)
            dq[block_at, q_lanes] = jnp.where(low, grad_q[:width], grad_q[width:])
            over = (((0,), (0,)), ((), ()))
            dk[keys_at, q_lanes] += lax.dot_general(grad_score, query2, over, preferred_element_type=f32)
            dv[keys_at, q_lanes] += lax.dot_general(weights, grad2, over, preferred_element_type=f32)
        return carry

    lax.fori_loop(0, QUERY_ROWS // 2, block, 0)
    for r in range(SIDE):
        own = pl.ds(r * SIDE, SIDE)
        at_query = pl.ds((r + 3) * QUERY_COLS, SIDE)
        at_key = pl.ds((r + 6) * KEY_COLS, SIDE)
        attn_out[own, :] = attn[at_query, :].astype(bf16)
        grads_out[own, :HALF] = (dq[at_query, :] * HEAD_DIM ** (-0.5)).astype(bf16)
        grads_out[own, HALF : 2 * HALF] = dk[at_key, :].astype(bf16)
        grads_out[own, 2 * HALF :] = dv[at_key, :].astype(bf16)


def attend(base, packed, grad_attention, alive, columns):
    vmem = pl.BlockSpec(memory_space=pltpu.VMEM)
    return pl.pallas_call(
        attention_kernel,
        out_shape=(
            jax.ShapeDtypeStruct((SIDE * SIDE, HALF), bf16),
            jax.ShapeDtypeStruct((SIDE * SIDE, 3 * HALF), bf16),
        ),
        in_specs=[pl.BlockSpec(memory_space=pltpu.SMEM), vmem, vmem, vmem, vmem],
        out_specs=(vmem, vmem),
        scratch_shapes=[
            pltpu.VMEM((KEY_ROWS * KEY_COLS, HALF), f32),
            pltpu.VMEM((KEY_ROWS * KEY_COLS, HALF), f32),
            pltpu.VMEM((QUERY_ROWS * QUERY_COLS, HALF), f32),
            pltpu.VMEM((QUERY_ROWS * QUERY_COLS, HALF), f32),
        ],
        compiler_params=pltpu.CompilerParams(vmem_limit_bytes=32 * 1024 * 1024),
        cost_estimate=pl.CostEstimate(flops=2 * 10**9, bytes_accessed=4 * 10**6, transcendentals=10**6),
    )(base, packed, grad_attention, alive, columns)


def feature_places(core, x, y, z):
    place = jnp.arange(D, dtype=jnp.int32)
    step = [(place // 24) % 4, (place // 96) % 4, place // 384]
    here = {"x": x, "y": y, "z": z}
    found = {}
    for name in ("x", "y", "z"):
        mine = [lax.rem(here[name] - step[STAGES[c].index(name)] + 4, 4) for c in range(2)]
        found[name] = jnp.where(core == 0, mine[0], mine[1])
    inner = place % 24
    high, low = found["z"] // 2, found["z"] % 2

    def owner(side):
        return (((high * 4 + found["y"]) * 2 + side) * 2 + low) * 4 + found["x"]

    feature_in = owner(inner // 12) * 12 + inner % 12
    row_out = owner(inner % 12 // 6) * 6 + inner % 6 + inner // 12 * DH
    return feature_in, row_out


def body(tiles, tissue, project_in, project_out, grad_layer):
    zh, y, core, zl, x = [lax.axis_index(name) for name in AXES]
    z = zh * 2 + zl
    tokens = 8 * SIDE
    contract_last = (((1,), (1,)), ((), ()))
    contract_first = (((0,), (0,)), ((), ()))

    halves = project_in.reshape(12, 3, 2, HALF)
    first, second = halves[:, :, 0].reshape(12, 3 * HALF), halves[:, :, 1].reshape(12, 3 * HALF)
    out_first, out_second = project_out[:, :DH], project_out[:, DH:]

    def shard(of_in, of_out):
        return jnp.concatenate([of_in, of_out.reshape(6, 2, HALF).transpose(1, 0, 2).reshape(12, HALF)], axis=1)

    shard_first, shard_second = shard(first, out_first), shard(second, out_second)
    mine = jnp.where(core == 0, shard_first, shard_second)
    other = swap_cores(jnp.where(core == 0, shard_second, shard_first))
    pair_in = by_core(core, mine[:, : 3 * HALF], other[:, : 3 * HALF], 0)
    mine_out, other_out = mine[:, 3 * HALF :].reshape(2, 6, HALF), other[:, 3 * HALF :].reshape(2, 6, HALF)
    pair_out = by_core(core, mine_out, other_out, 1).reshape(24, HALF)
    block = jnp.concatenate([pair_in, pair_out], axis=1)
    for stage in range(3):
        block = jnp.concatenate(gather_stage(block, stage), axis=0)
    weights_in, weights_out = block[:, : 3 * HALF], block[:, 3 * HALF :]

    flat_tiles = tiles.reshape(tokens, D).astype(f32)
    normed, inverse = normalize(flat_tiles)
    live = tissue.reshape(tokens, 1).astype(f32)
    grad_flat = grad_layer.reshape(tokens, D).astype(f32)
    tissue_lanes = jnp.broadcast_to(live.astype(bf16), (tokens, LANE))
    own_hidden = jnp.concatenate([normed.astype(bf16), tissue_lanes], axis=1).reshape(8, SIDE, D + LANE)
    own_grad = jnp.concatenate([(grad_flat * live).astype(bf16), tissue_lanes], axis=1).reshape(8, SIDE, D + LANE)
    sent = jnp.where(
        core == 1,
        jnp.concatenate([own_hidden[2:], own_grad[5:]], axis=0),
        jnp.concatenate([own_hidden[:6], own_grad[:3]], axis=0),
    )
    got = row_neighbour(sent)
    a = jnp.where(
        core == 0, jnp.concatenate([got[:6], own_hidden], axis=0), jnp.concatenate([own_hidden, got[:6]], axis=0)
    )
    b = jnp.where(
        core == 0, jnp.concatenate([got[6:], own_grad], axis=0), jnp.concatenate([own_grad, got[6:]], axis=0)
    )

    def columns_of(a_part, b_part):
        return jnp.concatenate([a_part.reshape(84, D + LANE), b_part.reshape(33, D + LANE)], axis=0)

    left = col_neighbour(columns_of(a[:, 10:], b[:, 13:]), 1)
    right = col_neighbour(columns_of(a[:, :6], b[:, :3]), -1)
    left_a, left_b = left[:84].reshape(14, 6, D + LANE), left[84:].reshape(11, 3, D + LANE)
    right_a, right_b = right[:84].reshape(14, 6, D + LANE), right[84:].reshape(11, 3, D + LANE)
    gap_a, gap_b = jnp.zeros((14, 2, D + LANE), bf16), jnp.zeros((11, 2, D + LANE), bf16)
    wide_a = jnp.concatenate(
        [a, left_a[:, 3:], right_a[:, :3], gap_a, left_a[:, :3], right_a[:, 3:], gap_a], axis=1
    ).reshape(14 * KEY_COLS, D + LANE)
    wide_b = jnp.concatenate([b, left_b, right_b, gap_b], axis=1).reshape(11 * QUERY_COLS, D + LANE)
    wide = jnp.concatenate([wide_a, wide_b], axis=0)
    wide_other = swap_cores(wide)
    all_a = by_core(core, wide[: 14 * KEY_COLS], wide_other[: 14 * KEY_COLS], 0)
    all_b = by_core(core, wide[14 * KEY_COLS :, :D], wide_other[14 * KEY_COLS :, :D], 0)
    alive_map = all_a[:, D].reshape(KEY_ROWS, KEY_COLS).astype(f32)

    feature_in, row_out = feature_places(core, x, y, z)
    order_in = (jnp.arange(D, dtype=jnp.int32)[:, None] == feature_in[None, :]).astype(bf16)
    order_out = (jnp.arange(2 * DH, dtype=jnp.int32)[:, None] == row_out[None, :]).astype(bf16)
    hidden = jnp.dot(all_a[:, :D], order_in, preferred_element_type=f32).astype(bf16)

    column_base = (zl * 4 + x) * SIDE
    j = jnp.arange(KEY_COLS, dtype=jnp.int32)
    key_col = jnp.select(
        [j < 16, j < 19, j < 22, j < 24, j < 27, j < 30],
        [j, j - 19, j - 3, j - 4000, j - 30, j - 8],
        -4000,
    )
    key_col = key_col + column_base
    col_start = jnp.clip(key_col[:QUERY_COLS] - 3, 0, GRID - WINDOW)[:, None]
    col_in = jnp.logical_and(key_col[None, :] >= col_start, key_col[None, :] < col_start + WINDOW)
    columns = jnp.tile(jnp.where(col_in, open_score, outside_score).astype(f32), (1, 8))
    alive = jnp.where(alive_map > 0, open_score, masked_score).astype(f32)
    alive = jnp.concatenate([alive[i : i + 21] for i in range(8)], axis=1)
    alive = jnp.concatenate([alive, alive[:3]], axis=0)
    row_base = ((zh * 4 + y) * SIDE).reshape(1)

    packed = jnp.dot(hidden, weights_in, preferred_element_type=f32).astype(bf16)
    natural = jnp.dot(order_out, weights_out, preferred_element_type=f32).astype(bf16)
    half_out = jnp.concatenate([natural[:DH], natural[DH:]], axis=1)
    mine_rows = lax.dynamic_slice_in_dim(half_out, core * HALF, HALF, axis=0)
    other_rows = swap_cores(lax.dynamic_slice_in_dim(half_out, (1 - core) * HALF, HALF, axis=0))
    rows_out = by_core(core, mine_rows, other_rows, 1)
    grad_attention = lax.dot_general(all_b, rows_out, contract_last, preferred_element_type=f32).astype(bf16)

    attention, grad_packed = attend(row_base, packed, grad_attention, alive, columns)

    hidden_own = hidden.reshape(KEY_ROWS, KEY_COLS, D)[6:22, :SIDE].reshape(SIDE * SIDE, D)
    grad_own = all_b.reshape(QUERY_ROWS, QUERY_COLS, D)[3:19, :SIDE].reshape(SIDE * SIDE, D)
    grad_own = lax.dynamic_slice_in_dim(grad_own, core * DH, DH, axis=1)
    attention_all = by_core(core, attention, swap_cores(attention), 1)
    grad_out = lax.dot_general(attention_all, grad_own, contract_first, preferred_element_type=f32).astype(bf16)
    grad_out = jnp.concatenate([grad_out[:, :HALF], grad_out[:, HALF:]], axis=0)
    grad_out = lax.dot_general(order_out, grad_out, contract_first, preferred_element_type=f32).astype(bf16)
    chunks = []
    for k in range(4):
        part = slice(k * 384, (k + 1) * 384)
        grad_in = lax.dot_general(
            hidden_own[:, part], grad_packed, contract_first, preferred_element_type=f32
        ).astype(bf16)
        chunks.append(jnp.concatenate([grad_in, grad_out[part]], axis=1))
    total = scatter_stage(chunks, 2)
    for stage in (1, 0):
        total = total.astype(bf16)
        size = total.shape[0] // 4
        total = scatter_stage([total[k * size : (k + 1) * size] for k in range(4)], stage)

    sums_in = total[:, : 3 * HALF].reshape(2, 12, 3 * HALF)
    sums_out = total[:, 3 * HALF :].reshape(2, 2, 6, HALF).transpose(1, 0, 2, 3).reshape(2, 12, HALF)
    sums = jnp.concatenate([sums_in, sums_out], axis=2)
    kept = jnp.where(core == 0, sums[0], sums[1])
    gotten = swap_cores(jnp.where(core == 0, sums[1], sums[0]))
    grad_project_in = by_core(
        core, kept[:, : 3 * HALF].reshape(12, 3, 1, HALF), gotten[:, : 3 * HALF].reshape(12, 3, 1, HALF), 2
    ).reshape(12, 3 * DH)
    kept_out = kept[:, 3 * HALF :].reshape(2, 6, HALF).transpose(1, 0, 2).reshape(6, DH)
    gotten_out = gotten[:, 3 * HALF :].reshape(2, 6, HALF).transpose(1, 0, 2).reshape(6, DH)
    grad_project_out = by_core(core, kept_out, gotten_out, 1)

    projected = jnp.dot(attention_all, half_out, preferred_element_type=f32)
    projected_mine = lax.dynamic_slice_in_dim(projected, core * tokens, tokens, axis=0)
    projected_other = swap_cores(lax.dynamic_slice_in_dim(projected, (1 - core) * tokens, tokens, axis=0))
    projected = by_core(core, projected_mine, projected_other, 1)
    layer_out = (flat_tiles + projected * live).astype(bf16).reshape(8, SIDE, D)

    grad_hidden = lax.dot_general(grad_packed, weights_in, contract_last, preferred_element_type=f32).astype(bf16)
    grad_hidden = lax.dot_general(grad_hidden, order_in, contract_last, preferred_element_type=f32)
    grad_hidden_mine = lax.dynamic_slice_in_dim(grad_hidden, core * tokens, tokens, axis=0)
    grad_hidden_other = swap_cores(
        lax.dynamic_slice_in_dim(grad_hidden, (1 - core) * tokens, tokens, axis=0).astype(bf16)
    )
    grad_hidden = grad_hidden_mine + grad_hidden_other.astype(f32)
    grad_norm = inverse * (
        grad_hidden
        - jnp.mean(grad_hidden, axis=-1, keepdims=True)
        - normed * jnp.mean(grad_hidden * normed, axis=-1, keepdims=True)
    )
    grad_tiles = (grad_flat + grad_norm).astype(bf16).reshape(8, SIDE, D)
    return (layer_out, grad_tiles, grad_project_in, grad_project_out)


def solution(mesh):
    fine = Mesh(mesh.devices.reshape(2, 4, 2, 2, 4), AXES)
    grid = P(("zh", "y", "c"), ("zl", "x"), None)
    rows = P(AXES, None)
    return jax.shard_map(
        body,
        mesh=fine,
        in_specs=(grid, P(("zh", "y", "c"), ("zl", "x")), rows, rows, grid),
        out_specs=(grid, grid, rows, rows),
        check_vma=False,
    )
```

time: 1530 us -> 232 us (0.15)
  waiting for transfers between devices: 609 us -> 42.7 us
  blocking collectives: 371 us -> 0 us
  starting transfers between devices: 234 us -> 72 us
  local copies, waits for them, and re-layouts: 196 us -> 34.2 us
  matrix products: 71.5 us -> 30.1 us
  Pallas kernels: 0 us -> 22.5 us
    all_gather x2 -> x0, waiting for transfers between devices: 586 us -> none  [the longest x1 308 us: body(): input_whole = lax.all_gather(project_in, ('row', 'col'), axis=0, tiled=True)]
    unnamed x1 -> x0, blocking collectives: 371 us -> none
    unnamed x64 -> x0, starting transfers between devices: 198 us -> none
    unnamed x147 -> x40, local copies, waits for them, and re-layouts: 116 us -> 11 us
    ppermute x12 -> x28, starting transfers between devices: 35.1 us -> 72 us  [the longest x18 42.5 us: shifted(): return lax.ppermute(value, AXES, stage_pairs(stage, shift))]
    ppermute x12 -> x28, waiting for transfers between devices: 7.22 us -> 42.7 us  [the longest x18 41 us: shifted(): return lax.ppermute(value, AXES, stage_pairs(stage, shift))]
    dynamic_slice x42 -> x1, local copies, waits for them, and re-layouts: 35 us -> 0.06 us  [body(): lax.dynamic_slice_in_dim(projected, core * tokens, tokens, axis=0)]
    dot_general x48 -> x12, matrix products: 62.7 us -> 30.1 us  [the longest x1 6.53 us: body(): jnp.dot(all_a[:, :D], order_in, preferred_element_type=f32).astype(bf16)]
  transfers between devices with their start and end apart: 78 -> 28, of which waited for: 9 -> 15; matrix products, arithmetic and copies ran while one was open for 5% -> 32% of each run, Pallas kernels for 0% -> 0%
where the time goes in v1:
time: 232 us; the launch traced here: 230 us
  starting transfers between devices  72 us (31%)
  waiting for transfers between devices  42.7 us (18%)
  local copies, waits for them, and re-layouts  34.2 us (15%)
  matrix products  30.1 us (13%)
  other arithmetic  26.3 us (11%)
  Pallas kernels  22.5 us (10%)
    ppermute x18, starting transfers between devices, shifted(): return lax.ppermute(value, AXES, stage_pairs(stage, shift))  42.5 us
    ppermute x18, waiting for transfers between devices, shifted(): return lax.ppermute(value, AXES, stage_pairs(stage, shift))  41 us
    pallas_call x1, Pallas kernels, attend(): pl.pallas_call(attention_kernel, out_shape=(jax.ShapeDtypeStruct((SIDE *...  22.5 us
    ppermute x7, starting transfers between devices, swap_cores(): return lax.ppermute(value, 'c', [(0, 1), (1, 0)])  21.7 us
    unnamed x40, local copies, waits for them, and re-layouts  11 us
    dot_general x1, matrix products, body(): jnp.dot(all_a[:, :D], order_in, preferred_element_type=f32).astype(bf16)  6.53 us
    dot_general x1, matrix products, body(): lax.dot_general(grad_hidden, order_in, contract_last, preferred_element_t...  6.18 us
    dot_general x1, matrix products, body(): jnp.dot(hidden, weights_in, preferred_element_type=f32).astype(bf16)  5.98 us
  transfers between devices with their start and end apart: 28, of which 15 were waited for; matrix products, arithmetic and copies ran while one was open for 32% of the time, Pallas kernels for 0%

profile of v1, /device:TPU:1, one launch (start us, length us, event | category | flops | bytes accessed | tf_op | source)
XLA Modules:
  0.0 229.7 jit_solution(11578510489304811035)
XLA Ops:
  5.8 4.6 %collective-permute-start = (bf16[9,16,1664]{2,1,0:T(8,128)(2,1)S(1)}, bf16[9,16,1664]{2,1,0:T(8,128)(2,1)S(1)}, u32[]{:S(2)}, u32[]{:S(2)}) collective-permute-start(bf16[9,16,1664]{2,1,0:T(8,128)(2,1)S(1)} %maximum_select_fusion.7), channel_id=1, source_target_pairs={{8,16},{16,8},{24,32},{32,24},{40,48},{48,40},{56,64},{64,56},{72,... | collective-permute-start | bytes 1437704 | tf_op jit(solution)/shard_map/ppermute | solution.py:60
  22.5 4.2 %collective-permute-start.9 = (bf16[96,1536]{1,0:T(8,128)(2,1)}, bf16[96,1536]{1,0:T(8,128)(2,1)}, u32[]{:S(2)}, u32[]{:S(2)}) collective-permute-start(bf16[96,1536]{1,0:T(8,128)(2,1)} %pad_maximum_fusion.9), channel_id=1, source_target_pairs={{0,32},{8,72},{4,36},{12,76},{64,96},{72,8},{68,100},{76,12},{16,4... | collective-permute-start | bytes 884744 | tf_op jit(solution)/shard_map/ppermute | solution.py:51
  40.1 7.4 %collective-permute-start.12 = (bf16[384,1536]{1,0:T(8,128)(2,1)}, bf16[384,1536]{1,0:T(8,128)(2,1)}, u32[]{:S(2)}, u32[]{:S(2)}) collective-permute-start(bf16[384,1536]{1,0:T(8,128)(2,1)} %get-tuple-element.52), channel_id=1, source_target_pairs={{0,2},{8,40},{4,6},{12,44},{64,66},{72,104},{68,70},{76,108},{16,1... | collective-permute-start | bytes 3538952 | tf_op jit(solution)/shard_map/ppermute | solution.py:51
  53.5 4.5 %concatenate.164 = bf16[14,32,1664]{2,1,0:T(8,128)(2,1)S(1)} concatenate(bf16[14,16,1664]{2,1,0:T(8,128)(2,1)S(1)} %maximum_select_fusion.5, bf16[14,3,1664]{2,1,0:T(4,128)(2,1)} %get-tuple-element.79, bf16[14,3,1664]{2,1,0:T(4,128)(2,1)} %get-tuple-element.46, bf16[14,2,1664]{2,1,0:T(2,128)(2,1)} %broadcast_in_dim.45, bf16[14,3,1664]{2,1,0:T(4,128)(2,1)} %get-tuple-element.80, ...), dimensions={1} | concatenate | bytes 2981888 | tf_op jit(solution)/shard_map/concatenate | solution.py:255
  59.6 5.3 %collective-permute-start.3 = (bf16[712,1664]{1,0:T(8,128)(2,1)}, bf16[712,1664]{1,0:T(8,128)(2,1)}, u32[]{:S(2)}, u32[]{:S(2)}) collective-permute-start(bf16[712,1664]{1,0:T(8,128)(2,1)} %pad_maximum_fusion), channel_id=1, source_target_pairs={{0,8},{8,0},{1,9},{9,1},{2,10},{10,2},{3,11},{11,3},{4,12},{12,4},... | collective-permute-start | bytes 7108616 | tf_op jit(solution)/shard_map/ppermute | solution.py:55
  70.8 3.5 %collective-permute-done.12 = bf16[384,1536]{1,0:T(8,128)(2,1)} collective-permute-done((bf16[384,1536]{1,0:T(8,128)(2,1)}, bf16[384,1536]{1,0:T(8,128)(2,1)}, u32[]{:S(2)}, u32[]{:S(2)}) %collective-permute-start.12) | collective-permute-done | bytes 1179680 | tf_op jit(solution)/shard_map/ppermute | solution.py:51
  76.6 4.1 %collective-permute-done.13 = bf16[384,1536]{1,0:T(8,128)(2,1)} collective-permute-done((bf16[384,1536]{1,0:T(8,128)(2,1)}, bf16[384,1536]{1,0:T(8,128)(2,1)}, u32[]{:S(2)}, u32[]{:S(2)}) %collective-permute-start.13) | collective-permute-done | bytes 1179680 | tf_op jit(solution)/shard_map/ppermute | solution.py:51
  83.1 3.5 %fusion.12 = bf16[1536,384]{0,1:T(8,128)(2,1)S(1)} fusion(s32[1536]{0:T(1024)S(1)} %fusion.79, bf16[1536,1536]{1,0:T(8,128)(2,1)} %constant_dynamic-update-slice_fusion.11), kind=kOutput, calls=%fused_computation.20 | convolution fusion | flops 1814888448 | bytes 2365440 | tf_op jit(solution)/shard_map/dot_general | solution.py:287
  90.8 4.0 %maximum_select_fusion = bf16[896,1664]{1,0:T(8,128)(2,1)S(1)} fusion(bf16[448,1664]{1,0:T(8,128)(2,1)S(1)} %slice.362, bf16[448,1664]{1,0:T(8,128)(2,1)S(1)} %bitcast.62, pred[]{:T(512)S(6)} %eq.25), kind=kLoop, calls=%fused_computation.15 | loop fusion | flops 13418496 | bytes 5963777 | tf_op jit(solution)/shard_map/jit(_where)/select_n | solution.py:83
  97.1 6.5 %fusion.8 = bf16[896,1536]{1,0:T(8,128)(2,1)S(1)} fusion(s32[1536]{0:T(1024)S(1)} %multiply_add_fusion, bf16[896,1664]{1,0:T(8,128)(2,1)} %copy-done.3), kind=kOutput, calls=%fused_computation.11 | convolution fusion | flops 4231593984 | bytes 5511168 | tf_op jit(solution)/shard_map/dot_general | solution.py:268
  105.7 6.0 %convolution_convert_fusion.packed_ref = bf16[896,1152]{1,0:T(8,128)(2,1)S(1)} fusion(bf16[896,1536]{1,0:T(8,128)(2,1)S(1)} %fusion.8, bf16[1536,1536]{1,0:T(8,128)(2,1)} %constant_dynamic-update-slice_fusion.11), kind=kOutput, calls=%fused_computation.10 | convolution fusion | flops 3171926016 | bytes 8355840 | tf_op jit(solution)/shard_map/dot_general | solution.py:286
  114.1 22.5 %shard_map.84 = (bf16[256,384]{1,0:T(8,128)(2,1)S(1)}, bf16[256,1152]{1,0:T(8,128)(2,1)S(1)}) custom-call(s32[1]{0:T(128)} %bitcast.base_ref, bf16[896,1152]{1,0:T(8,128)(2,1)S(1)} %convolution_convert_fusion.packed_ref, bf16[528,384]{1,0:T(8,128)(2,1)S(1)} %convolution_convert_fusion.6.grad_ref, f32[24,256]{1,0:T(8,128)S(1)} %pad_maximum_fusion.12.alive_ref, ...), custom_call_target="tpu_custom_call" | custom-call | flops 2000000000 | bytes 4000000 | tf_op jit(solution)/shard_map/pallas_call | solution.py:164
  137.7 10.0 %collective-permute-start.15 = (bf16[256,384]{1,0:T(8,128)(2,1)S(1)}, bf16[256,384]{1,0:T(8,128)(2,1)S(1)}, u32[]{:S(2)}, u32[]{:S(2)}) collective-permute-start(bf16[256,384]{1,0:T(8,128)(2,1)S(1)} %get-tuple-element.8), channel_id=1, source_target_pairs={{0,8},{8,0},{1,9},{9,1},{2,10},{10,2},{3,11},{11,3},{4,12},{12,4},... | collective-permute-start | bytes 589832 | tf_op jit(solution)/shard_map/ppermute | solution.py:55
  149.8 2.7 %fusion.13 = bf16[1536,384]{1,0:T(8,128)(2,1)S(1)} fusion(s32[1536]{0:T(1024)S(1)} %fusion.79, bf16[768,384]{1,0:T(8,128)(2,1)S(1)} %get-tuple-element.30, bf16[768,384]{1,0:T(8,128)(2,1)S(1)} %get-tuple-element.29), kind=kOutput, calls=%fused_computation.21 | convolution fusion | flops 1817247744 | bytes 2365440 | tf_op jit(solution)/shard_map/dot_general | solution.py:302
  153.6 16.1 %collective-permute-start.18 = (bf16[384,1536]{1,0:T(8,128)(2,1)}, bf16[384,1536]{1,0:T(8,128)(2,1)}, u32[]{:S(2)}, u32[]{:S(2)}) collective-permute-start(bf16[384,1536]{1,0:T(8,128)(2,1)} %pad_maximum_fusion.3), channel_id=1, source_target_pairs={{0,3},{8,56},{4,7},{12,60},{64,67},{72,120},{68,71},{76,124},{16,1... | collective-permute-start | bytes 3538952 | tf_op jit(solution)/shard_map/ppermute | solution.py:51
  172.6 6.2 %fusion.2 = f32[256,1536]{1,0:T(8,128)} fusion(s32[1536]{0:T(1024)S(1)} %multiply_add_fusion, bf16[256,1152]{1,0:T(8,128)(2,1)S(1)} %get-tuple-element.9, bf16[1536,1536]{1,0:T(8,128)(2,1)} %constant_dynamic-update-slice_fusion.11), kind=kOutput, calls=%fused_computation.4 | convolution fusion | flops 2116681728 | bytes 5707776 | tf_op jit(solution)/shard_map/dot_general | solution.py:335
  182.9 12.9 %collective-permute-done.18 = bf16[384,1536]{1,0:T(8,128)(2,1)} collective-permute-done((bf16[384,1536]{1,0:T(8,128)(2,1)}, bf16[384,1536]{1,0:T(8,128)(2,1)}, u32[]{:S(2)}, u32[]{:S(2)}) %collective-permute-start.18) | collective-permute-done | bytes 1179680 | tf_op jit(solution)/shard_map/ppermute | solution.py:51
  195.8 4.8 %collective-permute-done.20 = bf16[384,1536]{1,0:T(8,128)(2,1)} collective-permute-done((bf16[384,1536]{1,0:T(8,128)(2,1)}, bf16[384,1536]{1,0:T(8,128)(2,1)}, u32[]{:S(2)}, u32[]{:S(2)}) %collective-permute-start.20) | collective-permute-done | bytes 1179680 | tf_op jit(solution)/shard_map/ppermute | solution.py:51
  200.6 2.6 %add_convert_fusion = bf16[384,1536]{1,0:T(8,128)(2,1)S(1)} fusion(bf16[384,1536]{1,0:T(8,128)(2,1)} %collective-permute-done.20, bf16[384,1536]{1,0:T(8,128)(2,1)} %collective-permute-done.19, bf16[384,1536]{1,0:T(8,128)(2,1)} %collective-permute-done.18, bf16[384,384]{1,0:T(8,128)(2,1)S(1)} %get-tuple-element.25, ...), kind=kLoop, calls=%fused_computation.25 | loop fusion | flops 6488064 | bytes 5898240 | tf_op jit(solution)/shard_map/convert_element_type | solution.py:312
  204.8 4.4 %collective-permute-done.21 = bf16[96,1536]{1,0:T(8,128)(2,1)S(1)} collective-permute-done((bf16[96,1536]{1,0:T(8,128)(2,1)S(1)}, bf16[96,1536]{1,0:T(8,128)(2,1)S(1)}, u32[]{:S(2)}, u32[]{:S(2)}) %collective-permute-start.21) | collective-permute-done | bytes 294944 | tf_op jit(solution)/shard_map/ppermute | solution.py:51
  210.6 3.4 %collective-permute-done.23 = bf16[96,1536]{1,0:T(8,128)(2,1)S(1)} collective-permute-done((bf16[96,1536]{1,0:T(8,128)(2,1)S(1)}, bf16[96,1536]{1,0:T(8,128)(2,1)S(1)}, u32[]{:S(2)}, u32[]{:S(2)}) %collective-permute-start.23) | collective-permute-done | bytes 294944 | tf_op jit(solution)/shard_map/ppermute | solution.py:51
  214.1 3.2 %collective-permute-start.24 = (bf16[24,1536]{1,0:T(8,128)(2,1)S(1)}, bf16[24,1536]{1,0:T(8,128)(2,1)S(1)}, u32[]{:S(2)}, u32[]{:S(2)}) collective-permute-start(bf16[24,1536]{1,0:T(8,128)(2,1)S(1)} %get-tuple-element.49), channel_id=1, source_target_pairs={{0,68},{8,11},{4,0},{12,15},{64,4},{72,75},{68,64},{76,79},{16,84}... | collective-permute-start | bytes 221192 | tf_op jit(solution)/shard_map/ppermute | solution.py:51
  219.4 2.7 %collective-permute-done.25 = bf16[24,1536]{1,0:T(8,128)(2,1)S(1)} collective-permute-done((bf16[24,1536]{1,0:T(8,128)(2,1)S(1)}, bf16[24,1536]{1,0:T(8,128)(2,1)S(1)}, u32[]{:S(2)}, u32[]{:S(2)}) %collective-permute-start.25) | collective-permute-done | bytes 73760 | tf_op jit(solution)/shard_map/ppermute | solution.py:51
  222.7 4.2 %collective-permute-start.27 = (f32[12,1536]{1,0:T(8,128)S(1)}, f32[12,1536]{1,0:T(8,128)S(1)}, u32[]{:S(2)}, u32[]{:S(2)}) collective-permute-start(f32[12,1536]{1,0:T(8,128)S(1)} %get-tuple-element.59), channel_id=1, source_target_pairs={{0,8},{8,0},{1,9},{9,1},{2,10},{10,2},{3,11},{11,3},{4,12},{12,4},... | collective-permute-start | bytes 221192 | tf_op jit(solution)/shard_map/ppermute | solution.py:55
  (221 shorter events, 78.9 us)
Async XLA Ops:
  5.8 25.3 %collective-permute-start = (bf16[9,16,1664]{2,1,0:T(8,128)(2,1)S(1)}, bf16[9,16,1664]{2,1,0:T(8,128)(2,1)S(1)}, u32[]{:S(2)}, u32[]{:S(2)}) collective-permute-start(bf16[9,16,1664]{2,1,0:T(8,128)(2,1)S(1)} %maximum_select_fusion.7), channel_id=1, source_target_pairs={{8,16},{16,8},{24,32},{32,24},{40,48},{48,40},{56,64},{64,56},{72,... | collective-permute-start | bytes 1437704 | tf_op jit(solution)/shard_map/ppermute | solution.py:60
  13.0 5.4 %collective-permute-start.5 = (bf16[24,1536]{1,0:T(8,128)(2,1)S(1)}, bf16[24,1536]{1,0:T(8,128)(2,1)S(1)}, u32[]{:S(2)}, u32[]{:S(2)}) collective-permute-start(bf16[24,1536]{1,0:T(8,128)(2,1)S(1)} %get-tuple-element.70), channel_id=1, source_target_pairs={{0,4},{8,9},{4,64},{12,13},{64,68},{72,73},{68,0},{76,77},{16,20},... | collective-permute-start | bytes 221192 | tf_op jit(solution)/shard_map/ppermute | solution.py:51
  14.2 5.0 %collective-permute-start.6 = (bf16[24,1536]{1,0:T(8,128)(2,1)S(1)}, bf16[24,1536]{1,0:T(8,128)(2,1)S(1)}, u32[]{:S(2)}, u32[]{:S(2)}) collective-permute-start(bf16[24,1536]{1,0:T(8,128)(2,1)S(1)} %get-tuple-element.70), channel_id=1, source_target_pairs={{0,64},{8,10},{4,68},{12,14},{64,0},{72,74},{68,4},{76,78},{16,80}... | collective-permute-start | bytes 221192 | tf_op jit(solution)/shard_map/ppermute | solution.py:51
  20.9 9.3 %collective-permute-start.8 = (bf16[96,1536]{1,0:T(8,128)(2,1)}, bf16[96,1536]{1,0:T(8,128)(2,1)S(1)}, u32[]{:S(2)}, u32[]{:S(2)}) collective-permute-start(bf16[96,1536]{1,0:T(8,128)(2,1)} %pad_maximum_fusion.9), channel_id=1, source_target_pairs={{0,16},{8,12},{4,20},{12,72},{64,80},{72,76},{68,84},{76,8},{16,32... | collective-permute-start | bytes 884744 | tf_op jit(solution)/shard_map/ppermute | solution.py:51
  22.5 13.7 %collective-permute-start.9 = (bf16[96,1536]{1,0:T(8,128)(2,1)}, bf16[96,1536]{1,0:T(8,128)(2,1)}, u32[]{:S(2)}, u32[]{:S(2)}) collective-permute-start(bf16[96,1536]{1,0:T(8,128)(2,1)} %pad_maximum_fusion.9), channel_id=1, source_target_pairs={{0,32},{8,72},{4,36},{12,76},{64,96},{72,8},{68,100},{76,12},{16,4... | collective-permute-start | bytes 884744 | tf_op jit(solution)/shard_map/ppermute | solution.py:51
  26.8 11.3 %collective-permute-start.10 = (bf16[96,1536]{1,0:T(8,128)(2,1)}, bf16[96,1536]{1,0:T(8,128)(2,1)}, u32[]{:S(2)}, u32[]{:S(2)}) collective-permute-start(bf16[96,1536]{1,0:T(8,128)(2,1)} %pad_maximum_fusion.9), channel_id=1, source_target_pairs={{0,48},{8,76},{4,52},{12,8},{64,112},{72,12},{68,116},{76,72},{16,... | collective-permute-start | bytes 884744 | tf_op jit(solution)/shard_map/ppermute | solution.py:51
  32.7 14.7 %collective-permute-start.1 = (bf16[117,1664]{1,0:T(8,128)(2,1)}, bf16[117,1664]{1,0:T(8,128)(2,1)S(1)}, u32[]{:S(2)}, u32[]{:S(2)}) collective-permute-start(bf16[117,1664]{1,0:T(8,128)(2,1)} %pad_maximum_fusion.6), channel_id=1, source_target_pairs={{0,1},{1,2},{2,3},{3,4},{4,5},{5,6},{6,7},{8,9},{9,10},{10,11},{11... | collective-permute-start | bytes 1168136 | tf_op jit(solution)/shard_map/ppermute | solution.py:65
  35.0 12.6 %collective-permute-start.2 = (bf16[117,1664]{1,0:T(8,128)(2,1)S(1)}, bf16[117,1664]{1,0:T(8,128)(2,1)}, u32[]{:S(2)}, u32[]{:S(2)}) collective-permute-start(bf16[117,1664]{1,0:T(8,128)(2,1)S(1)} %pad_maximum_fusion.7), channel_id=1, source_target_pairs={{1,0},{2,1},{3,2},{4,3},{5,4},{6,5},{7,6},{9,8},{10,9},{11,10},{12... | collective-permute-start | bytes 1168136 | tf_op jit(solution)/shard_map/ppermute | solution.py:65
  40.0 28.5 %collective-permute-start.11 = (bf16[384,1536]{1,0:T(8,128)(2,1)}, bf16[384,1536]{1,0:T(8,128)(2,1)}, u32[]{:S(2)}, u32[]{:S(2)}) collective-permute-start(bf16[384,1536]{1,0:T(8,128)(2,1)} %get-tuple-element.52), channel_id=1, source_target_pairs={{0,1},{8,24},{4,5},{12,28},{64,65},{72,88},{68,69},{76,92},{16,17}... | collective-permute-start | bytes 3538952 | tf_op jit(solution)/shard_map/ppermute | solution.py:51
  40.1 34.2 %collective-permute-start.12 = (bf16[384,1536]{1,0:T(8,128)(2,1)}, bf16[384,1536]{1,0:T(8,128)(2,1)}, u32[]{:S(2)}, u32[]{:S(2)}) collective-permute-start(bf16[384,1536]{1,0:T(8,128)(2,1)} %get-tuple-element.52), channel_id=1, source_target_pairs={{0,2},{8,40},{4,6},{12,44},{64,66},{72,104},{68,70},{76,108},{16,1... | collective-permute-start | bytes 3538952 | tf_op jit(solution)/shard_map/ppermute | solution.py:51
  59.6 29.8 %collective-permute-start.3 = (bf16[712,1664]{1,0:T(8,128)(2,1)}, bf16[712,1664]{1,0:T(8,128)(2,1)}, u32[]{:S(2)}, u32[]{:S(2)}) collective-permute-start(bf16[712,1664]{1,0:T(8,128)(2,1)} %pad_maximum_fusion), channel_id=1, source_target_pairs={{0,8},{8,0},{1,9},{9,1},{2,10},{10,2},{3,11},{11,3},{4,12},{12,4},... | collective-permute-start | bytes 7108616 | tf_op jit(solution)/shard_map/ppermute | solution.py:55
  64.8 15.9 %collective-permute-start.13 = (bf16[384,1536]{1,0:T(8,128)(2,1)}, bf16[384,1536]{1,0:T(8,128)(2,1)}, u32[]{:S(2)}, u32[]{:S(2)}) collective-permute-start(bf16[384,1536]{1,0:T(8,128)(2,1)} %get-tuple-element.52), channel_id=1, source_target_pairs={{0,3},{8,56},{4,7},{12,60},{64,67},{72,120},{68,71},{76,124},{16,1... | collective-permute-start | bytes 3538952 | tf_op jit(solution)/shard_map/ppermute | solution.py:51
  87.9 23.9 %collective-permute-start.14 = (bf16[384,768]{0,1:T(8,128)(2,1)}, bf16[384,768]{0,1:T(8,128)(2,1)}, u32[]{:S(2)}, u32[]{:S(2)}) collective-permute-start(bf16[384,768]{0,1:T(8,128)(2,1)} %get-tuple-element.32), channel_id=1, source_target_pairs={{0,8},{8,0},{1,9},{9,1},{2,10},{10,2},{3,11},{11,3},{4,12},{12,4},... | collective-permute-start | bytes 1769480 | tf_op jit(solution)/shard_map/ppermute | solution.py:55
  137.7 11.4 %collective-permute-start.15 = (bf16[256,384]{1,0:T(8,128)(2,1)S(1)}, bf16[256,384]{1,0:T(8,128)(2,1)S(1)}, u32[]{:S(2)}, u32[]{:S(2)}) collective-permute-start(bf16[256,384]{1,0:T(8,128)(2,1)S(1)} %get-tuple-element.8), channel_id=1, source_target_pairs={{0,8},{8,0},{1,9},{9,1},{2,10},{10,2},{3,11},{11,3},{4,12},{12,4},... | collective-permute-start | bytes 589832 | tf_op jit(solution)/shard_map/ppermute | solution.py:55
  153.6 42.2 %collective-permute-start.18 = (bf16[384,1536]{1,0:T(8,128)(2,1)}, bf16[384,1536]{1,0:T(8,128)(2,1)}, u32[]{:S(2)}, u32[]{:S(2)}) collective-permute-start(bf16[384,1536]{1,0:T(8,128)(2,1)} %pad_maximum_fusion.3), channel_id=1, source_target_pairs={{0,3},{8,56},{4,7},{12,60},{64,67},{72,120},{68,71},{76,124},{16,1... | collective-permute-start | bytes 3538952 | tf_op jit(solution)/shard_map/ppermute | solution.py:51
  170.8 25.0 %collective-permute-start.19 = (bf16[384,1536]{1,0:T(8,128)(2,1)}, bf16[384,1536]{1,0:T(8,128)(2,1)}, u32[]{:S(2)}, u32[]{:S(2)}) collective-permute-start(bf16[384,1536]{1,0:T(8,128)(2,1)} %pad_maximum_fusion.4), channel_id=1, source_target_pairs={{0,2},{8,40},{4,6},{12,44},{64,66},{72,104},{68,70},{76,108},{16,1... | collective-permute-start | bytes 3538952 | tf_op jit(solution)/shard_map/ppermute | solution.py:51
  172.0 28.6 %collective-permute-start.20 = (bf16[384,1536]{1,0:T(8,128)(2,1)}, bf16[384,1536]{1,0:T(8,128)(2,1)}, u32[]{:S(2)}, u32[]{:S(2)}) collective-permute-start(bf16[384,1536]{1,0:T(8,128)(2,1)} %pad_maximum_fusion.5), channel_id=1, source_target_pairs={{0,1},{8,24},{4,5},{12,28},{64,65},{72,88},{68,69},{76,92},{16,17}... | collective-permute-start | bytes 3538952 | tf_op jit(solution)/shard_map/ppermute | solution.py:51
  181.3 45.7 %collective-permute-start.16 = (f32[128,768]{1,0:T(8,128)S(1)}, f32[128,768]{1,0:T(8,128)S(1)}, u32[]{:S(2)}, u32[]{:S(2)}) collective-permute-start(f32[128,768]{1,0:T(8,128)S(1)} %get-tuple-element.36), channel_id=1, source_target_pairs={{0,8},{8,0},{1,9},{9,1},{2,10},{10,2},{3,11},{11,3},{4,12},{12,4},... | collective-permute-start | bytes 1179656 | tf_op jit(solution)/shard_map/ppermute | solution.py:55
  203.3 5.9 %collective-permute-start.21 = (bf16[96,1536]{1,0:T(8,128)(2,1)S(1)}, bf16[96,1536]{1,0:T(8,128)(2,1)S(1)}, u32[]{:S(2)}, u32[]{:S(2)}) collective-permute-start(bf16[96,1536]{1,0:T(8,128)(2,1)S(1)} %get-tuple-element.22), channel_id=1, source_target_pairs={{0,48},{8,76},{4,52},{12,8},{64,112},{72,12},{68,116},{76,72},{16,... | collective-permute-start | bytes 884744 | tf_op jit(solution)/shard_map/ppermute | solution.py:51
  203.4 7.3 %collective-permute-start.22 = (bf16[96,1536]{1,0:T(8,128)(2,1)S(1)}, bf16[96,1536]{1,0:T(8,128)(2,1)S(1)}, u32[]{:S(2)}, u32[]{:S(2)}) collective-permute-start(bf16[96,1536]{1,0:T(8,128)(2,1)S(1)} %get-tuple-element.24), channel_id=1, source_target_pairs={{0,32},{8,72},{4,36},{12,76},{64,96},{72,8},{68,100},{76,12},{16,4... | collective-permute-start | bytes 884744 | tf_op jit(solution)/shard_map/ppermute | solution.py:51
  203.9 10.0 %collective-permute-start.23 = (bf16[96,1536]{1,0:T(8,128)(2,1)S(1)}, bf16[96,1536]{1,0:T(8,128)(2,1)S(1)}, u32[]{:S(2)}, u32[]{:S(2)}) collective-permute-start(bf16[96,1536]{1,0:T(8,128)(2,1)S(1)} %get-tuple-element.23), channel_id=1, source_target_pairs={{0,16},{8,12},{4,20},{12,72},{64,80},{72,76},{68,84},{76,8},{16,32... | collective-permute-start | bytes 884744 | tf_op jit(solution)/shard_map/ppermute | solution.py:51
  214.1 5.3 %collective-permute-start.24 = (bf16[24,1536]{1,0:T(8,128)(2,1)S(1)}, bf16[24,1536]{1,0:T(8,128)(2,1)S(1)}, u32[]{:S(2)}, u32[]{:S(2)}) collective-permute-start(bf16[24,1536]{1,0:T(8,128)(2,1)S(1)} %get-tuple-element.49), channel_id=1, source_target_pairs={{0,68},{8,11},{4,0},{12,15},{64,4},{72,75},{68,64},{76,79},{16,84}... | collective-permute-start | bytes 221192 | tf_op jit(solution)/shard_map/ppermute | solution.py:51
  217.3 5.2 %collective-permute-start.26 = (bf16[24,1536]{1,0:T(8,128)(2,1)S(1)}, bf16[24,1536]{1,0:T(8,128)(2,1)S(1)}, u32[]{:S(2)}, u32[]{:S(2)}) collective-permute-start(bf16[24,1536]{1,0:T(8,128)(2,1)S(1)} %get-tuple-element.50), channel_id=1, source_target_pairs={{0,4},{8,9},{4,64},{12,13},{64,68},{72,73},{68,0},{76,77},{16,20},... | collective-permute-start | bytes 221192 | tf_op jit(solution)/shard_map/ppermute | solution.py:51
  222.7 5.2 %collective-permute-start.27 = (f32[12,1536]{1,0:T(8,128)S(1)}, f32[12,1536]{1,0:T(8,128)S(1)}, u32[]{:S(2)}, u32[]{:S(2)}) collective-permute-start(f32[12,1536]{1,0:T(8,128)S(1)} %get-tuple-element.59), channel_id=1, source_target_pairs={{0,8},{8,0},{1,9},{9,1},{2,10},{10,2},{3,11},{11,3},{4,12},{12,4},... | collective-permute-start | bytes 221192 | tf_op jit(solution)/shard_map/ppermute | solution.py:55
  (17 other events, 65.6 us)
